TPU v7x, 32 devices: a whole 2x2x4 slice. The times are simulated.
32 devices in a mesh: seq: 8 (over z, x), mp: 4 (over y, core).
Axes of the slice: x: 2, y: 2, z: 4, core: 2. Of those that a mesh axis runs over, the one named last changes fastest.
Arguments:
- states: bfloat16 [4, 16, 2560], P(None, 'seq', 'mp'), may hold values from -6 to 6
- norm_gain: float32 [2560], replicated, may hold values from 0.5 to 2
- query_gain: float32 [128], replicated, may hold values from 0.7 to 2
- key_gain: float32 [128], replicated, may hold values from 0.7 to 2
- w_query: bfloat16 [2560, 2048], P(None, 'mp'), may hold values from -0.125 to 0.125
- key_matrix: bfloat16 [2560, 512], P(None, 'mp'), may hold values from -0.125 to 0.125
- value_matrix: bfloat16 [2560, 512], P(None, 'mp'), may hold values from -0.125 to 0.125
- w_out: bfloat16 [2048, 2560], P('mp'), may hold values from -0.125 to 0.125
- cached_key_blocks: bfloat16 [128, 256, 512], P('seq', None, 'mp'), may hold values from -216 to 216
- cached_value_blocks: bfloat16 [128, 256, 512], P('seq', None, 'mp'), may hold values from -6 to 6
- req_len: int32 [16], replicated, may hold values from 1 to 2048, as said below
- slot_request: int32 [128], P('seq'), may hold values from 0 to 15, as said below
- slot_block: int32 [128], P('seq'), may hold values from 0 to 7
- slot_empty: int32 [128], P('seq'), may hold values from 0 to 1
Outputs:
- hidden: bfloat16 [4, 16, 2560], P(None, 'seq', 'mp')
- new_keys: bfloat16 [4, 16, 512], P(None, 'seq', 'mp')
- new_values: bfloat16 [4, 16, 512], P(None, 'seq', 'mp')
Inputs may be any that keep to these rules, and one draw needn't show every extreme that they name: `req_len`: exactly 12 requests have length 2048; each other request has length at most 511, and one of them exactly that. Slot s holds positions slot_block[s] * 256 onward of request slot_request[s] unless slot_empty[s] = 1. Each block of a request below its length lies in exactly one slot that is not empty. A request of length 2048 has one block on every index of seq; every block of any other request b lies on index b // 2 of seq.
All inputs are finite; a program needn't handle non-finite values.
Results may differ from a plain program's by a relative error of at most 0.0098.
Values may be sent and summed in bfloat16 or wider, within the bound.
A program may use at most 64 MiB of HBM per device.

v0:
```python
import jax
import jax.numpy as jnp
from jax import lax
from jax.sharding import PartitionSpec as P

HEAD_SIZE = 128
STEPS = 4


ROPE_BASE = 1000000.0
NEGATIVE = -1e30
HIGHEST = lax.Precision.HIGHEST


def scaled_rms(values, gain):
    return values * lax.rsqrt(jnp.mean(values * values, axis=-1, keepdims=True) + 1e-06) * gain


def rotate(values, positions):
    halfway = values.shape[-1] // 2
    frequency = ROPE_BASE ** (-(jnp.arange(halfway, dtype=jnp.float32) * 2.0) / values.shape[-1])
    angles = positions.astype(jnp.float32)[..., None, None] * frequency
    cosine = jnp.cos(angles)
    sine_part = jnp.sin(angles)
    leading = values[..., :halfway]
    trailing = values[..., halfway:]
    return jnp.concatenate(
        [leading * cosine - trailing * sine_part, trailing * cosine + leading * sine_part], axis=-1
    )


def project(inputs, positions, norm_gain, query_gain, key_gain, w_query, key_matrix, value_matrix):
    number = inputs.shape[0]
    normed = scaled_rms(inputs.astype(jnp.float32), norm_gain).astype(jnp.bfloat16)
    query_rows = jnp.dot(normed, w_query, preferred_element_type=jnp.float32).reshape(
        number, -1, HEAD_SIZE
    )
    keys = jnp.dot(normed, key_matrix, preferred_element_type=jnp.float32).reshape(
        number, -1, HEAD_SIZE
    )
    values = jnp.dot(normed, value_matrix, preferred_element_type=jnp.float32).astype(jnp.bfloat16)
    query_rows = (
        rotate(scaled_rms(query_rows, query_gain), positions)
        .reshape(number, -1)
        .astype(jnp.bfloat16)
    )
    keys = rotate(scaled_rms(keys, key_gain), positions).reshape(number, -1).astype(jnp.bfloat16)
    return (query_rows, keys, values)


def shards(
    states,
    norm_gain,
    query_gain,
    key_gain,
    w_query,
    key_matrix,
    value_matrix,
    w_out,
    cached_key_blocks,
    cached_value_blocks,
    req_len,
    slot_request,
    slot_block,
    slot_empty,
):
    own_rows = states.shape[1]
    first_row = lax.axis_index("seq") * own_rows
    kv_heads = key_matrix.shape[1] // HEAD_SIZE
    q_heads = w_query.shape[1] // HEAD_SIZE
    head_sharing = q_heads // kv_heads
    query_width = w_query.shape[1]
    kv_width = key_matrix.shape[1]
    slot_count = cached_key_blocks.shape[0]
    block_len = cached_key_blocks.shape[1]
    requests = req_len.shape[0]
    scaling = HEAD_SIZE ** (-0.5)
    slot_len = jnp.take(req_len, slot_request)
    offsets = jnp.arange(block_len, dtype=jnp.int32)
    filled = (slot_empty[:, None] == 0) & (
        slot_block[:, None] * block_len + offsets[None, :] < slot_len[:, None]
    )
    filled_wide = filled[None, :, None, None, :]
    belongs = (slot_request[None, :] == jnp.arange(requests, dtype=jnp.int32)[:, None]) & (
        slot_empty[None, :] == 0
    )
    belongs_float = belongs.astype(jnp.float32)
    keys_split = cached_key_blocks.reshape(slot_count, block_len, kv_heads, HEAD_SIZE)
    values_split = cached_value_blocks.reshape(slot_count, block_len, kv_heads, HEAD_SIZE)
    turn_spans = [(sequence_index, sequence_index + 1) for sequence_index in range(STEPS)]
    past_keys = []
    past_values = []
    results = []
    for low_turn, high_turn in turn_spans:
        number = high_turn - low_turn
        turn_ids = jnp.arange(low_turn, high_turn, dtype=jnp.int32)
        block_states = states[low_turn:high_turn]
        wide_states = lax.all_gather(block_states, "mp", axis=2, tiled=True)
        portion = lax.all_gather(wide_states, "seq", axis=1, tiled=True)
        portion_rows = portion.shape[1]
        portion_positions = req_len[None, :] + turn_ids[:, None]
        part_query, part_key, part_value = project(
            portion.reshape(number * portion_rows, -1),
            portion_positions.reshape(-1),
            norm_gain,
            query_gain,
            key_gain,
            w_query,
            key_matrix,
            value_matrix,
        )
        everyone = jnp.concatenate([part_query, part_key, part_value], axis=1).reshape(
            number, portion_rows, -1
        )
        own_packed = lax.dynamic_slice_in_dim(everyone, first_row, own_rows, 1)
        all_query = everyone[:, :, :query_width]
        own_heads = own_packed[:, :, :query_width].reshape(
            number, own_rows, kv_heads, head_sharing, HEAD_SIZE
        )
        past_keys.append(own_packed[:, :, query_width : query_width + kv_width])
        past_values.append(own_packed[:, :, query_width + kv_width :])
        slot_query = jnp.take(all_query, slot_request, axis=1).reshape(
            number, slot_count, kv_heads, head_sharing, HEAD_SIZE
        )
        scores = (
            jnp.einsum(
                "tsngd,sknd->tsngk", slot_query, keys_split, preferred_element_type=jnp.float32
            )
            * scaling
        )
        slot_maximum = jnp.max(jnp.where(filled_wide, scores, NEGATIVE), axis=-1)
        row_top = jnp.max(
            jnp.where(belongs[None, :, :, None, None], slot_maximum[:, None], NEGATIVE), axis=2
        )
        slot_reference = jnp.take(row_top, slot_request, axis=1)
        weights = jnp.where(
            filled_wide,
            jnp.exp(jnp.where(filled_wide, scores - slot_reference[..., None], 0.0)),
            0.0,
        )
        slot_total = jnp.sum(weights, axis=-1)
        slot_mix = jnp.einsum(
            "tsngk,sknd->tsngd",
            weights.astype(jnp.bfloat16),
            values_split,
            preferred_element_type=jnp.float32,
        )
        row_total = jnp.einsum("bs,tsng->tbng", belongs_float, slot_total, precision=HIGHEST)
        row_mix = jnp.einsum("bs,tsngd->tbngd", belongs_float, slot_mix, precision=HIGHEST)
        every_top = lax.pmax(row_top, "seq")
        every_factor = jnp.exp(row_top - every_top)
        summed_total, summed_mix = lax.psum(
            (row_total * every_factor, row_mix * every_factor[..., None]), "seq"
        )
        own_top = lax.dynamic_slice_in_dim(every_top, first_row, own_rows, 1)
        own_total = lax.dynamic_slice_in_dim(summed_total, first_row, own_rows, 1)
        own_mix = lax.dynamic_slice_in_dim(summed_mix, first_row, own_rows, 1)
        earlier_keys = jnp.concatenate(past_keys, axis=0).reshape(
            high_turn, own_rows, kv_heads, HEAD_SIZE
        )
        earlier_values = jnp.concatenate(past_values, axis=0).reshape(
            high_turn, own_rows, kv_heads, HEAD_SIZE
        )
        fresh_scores = (
            jnp.einsum(
                "trngd,jrnd->trngj", own_heads, earlier_keys, preferred_element_type=jnp.float32
            )
            * scaling
        )
        allowed = (jnp.arange(high_turn, dtype=jnp.int32)[None, :] <= turn_ids[:, None])[
            :, None, None, None, :
        ]
        fresh_top = jnp.max(jnp.where(allowed, fresh_scores, NEGATIVE), axis=-1)
        overall = jnp.maximum(own_top, fresh_top)
        retained = jnp.exp(own_top - overall)
        fresh_weights = jnp.where(
            allowed, jnp.exp(jnp.where(allowed, fresh_scores - overall[..., None], 0.0)), 0.0
        )
        denominator = own_total * retained + jnp.sum(fresh_weights, axis=-1)
        mixture = own_mix * retained[..., None] + jnp.einsum(
            "trngj,jrnd->trngd",
            fresh_weights.astype(jnp.bfloat16),
            earlier_values,
            preferred_element_type=jnp.float32,
        )
        attended = (
            (mixture / denominator[..., None])
            .astype(jnp.bfloat16)
            .reshape(number * own_rows, query_width)
        )
        projected_out = jnp.dot(attended, w_out, preferred_element_type=jnp.float32).reshape(
            number, own_rows, -1
        )
        summed = lax.psum_scatter(projected_out, "mp", scatter_dimension=2, tiled=True)
        results.append((block_states.astype(jnp.float32) + summed).astype(jnp.bfloat16))
    return (
        jnp.concatenate(results, axis=0),
        jnp.concatenate(past_keys, axis=0),
        jnp.concatenate(past_values, axis=0),
    )


def solution(mesh):
    placed = (
        P(None, "seq", "mp"),
        P(),
        P(),
        P(),
        P(None, "mp"),
        P(None, "mp"),
        P(None, "mp"),
        P("mp", None),
        P("seq", None, "mp"),
        P("seq", None, "mp"),
        P(),
        P("seq"),
        P("seq"),
        P("seq"),
    )
    return jax.shard_map(
        shards,
        mesh=mesh,
        in_specs=placed,
        out_specs=(P(None, "seq", "mp"), P(None, "seq", "mp"), P(None, "seq", "mp")),
        check_vma=False,
    )
```

profile of v0, /device:TPU:0, one launch (start us, length us, event | category | flops | bytes accessed | tf_op | source)
XLA Modules:
  0.0 415.3 jit_solution(15635874871319568021)
XLA Ops:
  7.3 0.5 multiply_power_fusion
  7.8 0.7 fusion.245
  8.6 6.2 %all_gather.28 = bf16[1,2,2560]{2,0,1:T(2,128)(2,1)S(1)} all-gather(bf16[1,2,640]{2,0,1:T(2,128)(2,1)S(1)} %copy.423), channel_id=1, replica_groups=mesh['seq'=8,'mp'=4] {'mp'}, dimensions={2}, use_global_device_ids=true | all-gather | bytes 12800 | tf_op jit(solution)/shard_map/all_gather | solution.py:98
  14.7 5.4 %all_gather.24 = bf16[1,2,2560]{2,0,1:T(2,128)(2,1)S(1)} all-gather(bf16[1,2,640]{2,0,1:T(2,128)(2,1)S(1)} %copy.417), channel_id=1, replica_groups=mesh['seq'=8,'mp'=4] {'mp'}, dimensions={2}, use_global_device_ids=true | all-gather | bytes 12800 | tf_op jit(solution)/shard_map/all_gather | solution.py:98
  20.1 31.1 %all_gather.25 = bf16[1,16,2560]{2,0,1:T(2,128)(2,1)S(1)} all-gather(bf16[1,2,2560]{2,0,1:T(2,128)(2,1)S(1)} %all_gather.24), channel_id=1, replica_groups=mesh['seq'=8,'mp'=4] {'seq'}, dimensions={1}, use_global_device_ids=true | all-gather | bytes 92160 | tf_op jit(solution)/shard_map/all_gather | solution.py:99
  51.6 2.0 convolution_convert_fusion.3
  53.5 2.0 multiply_reduce_fusion.7
  55.5 30.6 %all_gather.29 = bf16[1,16,2560]{2,0,1:T(2,128)(2,1)S(1)} all-gather(bf16[1,2,2560]{2,0,1:T(2,128)(2,1)S(1)} %all_gather.28), channel_id=1, replica_groups=mesh['seq'=8,'mp'=4] {'seq'}, dimensions={1}, use_global_device_ids=true | all-gather | bytes 92160 | tf_op jit(solution)/shard_map/all_gather | solution.py:99
  86.3 0.9 convolution_convert_fusion.1
  87.1 0.9 multiply_reduce_fusion.5
  88.0 5.2 %all_gather.26 = bf16[1,2,2560]{2,0,1:T(2,128)(2,1)S(1)} all-gather(bf16[1,2,640]{2,0,1:T(2,128)(2,1)S(1)} %copy.420), channel_id=1, replica_groups=mesh['seq'=8,'mp'=4] {'mp'}, dimensions={2}, use_global_device_ids=true | all-gather | bytes 12800 | tf_op jit(solution)/shard_map/all_gather | solution.py:98
  93.2 30.6 %all_gather.27 = bf16[1,16,2560]{2,0,1:T(2,128)(2,1)S(1)} all-gather(bf16[1,2,2560]{2,0,1:T(2,128)(2,1)S(1)} %all_gather.26), channel_id=1, replica_groups=mesh['seq'=8,'mp'=4] {'seq'}, dimensions={1}, use_global_device_ids=true | all-gather | bytes 92160 | tf_op jit(solution)/shard_map/all_gather | solution.py:99
  123.9 0.9 convolution_convert_fusion.2
  124.8 1.5 multiply_reduce_fusion.6
  126.3 5.2 %all_gather.30 = bf16[1,2,2560]{2,0,1:T(2,128)(2,1)S(1)} all-gather(bf16[1,2,640]{2,0,1:T(2,128)(2,1)S(1)} %copy.426), channel_id=1, replica_groups=mesh['seq'=8,'mp'=4] {'mp'}, dimensions={2}, use_global_device_ids=true | all-gather | bytes 12800 | tf_op jit(solution)/shard_map/all_gather | solution.py:98
  131.4 30.6 %all_gather.31 = bf16[1,16,2560]{2,0,1:T(2,128)(2,1)S(1)} all-gather(bf16[1,2,2560]{2,0,1:T(2,128)(2,1)S(1)} %all_gather.30), channel_id=1, replica_groups=mesh['seq'=8,'mp'=4] {'seq'}, dimensions={1}, use_global_device_ids=true | all-gather | bytes 92160 | tf_op jit(solution)/shard_map/all_gather | solution.py:99
  162.2 0.8 convolution_convert_fusion
  163.4 4.4 %copy.411 = bf16[512,2560]{1,0:T(8,128)(2,1)} copy(bf16[512,2560]{0,1:T(8,128)(2,1)} %bitcast.570) | data formatting | bytes 5242880 | tf_op jit(solution)/shard_map/dot_general | solution.py:35
  167.8 2.8 multiply_reduce_fusion.3
  170.7 0.9 multiply_reduce_fusion
  171.7 0.9 multiply_reduce_fusion.1
  172.6 0.9 multiply_reduce_fusion.2
  173.6 0.7 gather_fusion
  175.4 0.6 gather_fusion.7
  176.3 0.6 gather_fusion.5
  177.1 0.6 gather_fusion.3
  178.0 0.6 gather_fusion.1
  178.7 1.7 fusion.1
  180.4 1.6 fusion.2
  182.0 1.6 fusion
  183.8 0.5 select_reduce_fusion.3
  184.8 0.6 gather_fusion.2
  185.5 0.6 gather_fusion.8
  186.2 0.6 gather_fusion.4
  186.9 0.6 gather_fusion.6
  187.9 1.6 fusion.62
  189.5 1.5 fusion.65
  191.1 1.5 fusion.68
  193.2 21.5 %all-reduce.1 = (f32[1,16,1,4]{1,3,2,0:T(4,128)S(1)}, f32[1,16,1,4]{1,3,2,0:T(4,128)S(1)}, f32[1,16,1,4]{1,3,2,0:T(4,128)S(1)}, f32[1,16,1,4]{1,3,2,0:T(4,128)S(1)}) all-reduce(f32[1,16,1,4]{1,3,2,0:T(4,128)S(1)} %bitcast.578, f32[1,16,1,4]{1,3,2,0:T(4,128)S(1)} %bitcast.577, ...), channel_id=1, replica_groups=mesh['seq'=8,'mp'=4] {'seq'}, use_global_device_ids=true, to_apply=%region_39.42 | all-reduce | flops 256 | bytes 2048 | tf_op jit(solution)/shard_map/pmax | solution.py:150
  214.8 0.8 fusion.9
  215.6 0.8 fusion.10
  216.4 0.8 fusion.12
  217.2 0.8 fusion.11
  217.9 0.7 fusion.4
  218.7 0.7 fusion.7
  219.4 0.7 fusion.6
  220.2 0.7 fusion.5
  224.6 65.4 %all-reduce.4.cloned.1.call-done = (f32[1,16,1,4,128]{4,1,3,2,0:T(8,128)}, f32[1,16,1,4]{1,3,2,0:T(4,128)}, f32[1,16,1,4,128]{4,1,3,2,0:T(8,128)}, f32[1,16,1,4]...) async-done(((f32[1,16,1,4,128]{4,1,3,2,0:T(8,128)}, ...) | async-done | bytes 132112 | tf_op jit(solution)/shard_map/psum | solution.py:152
  290.0 0.8 fusion.160
  290.8 3.0 convolution_bitcast_fusion
  294.1 3.0 convolution_bitcast_fusion.1
  297.2 3.0 convolution_bitcast_fusion.2
  300.4 3.0 convolution_bitcast_fusion.3
  303.4 0.6 copy.392
  304.0 0.6 copy.391
  304.5 15.2 %reduce-scatter.19.cloned.1.call-done = f32[640,2]{1,0:T(8,128)} async-done(((f32[2560,2]{1,0:T(8,128)}), f32[640,2]{1,0:T(8,128)}) %reduce-scatter.19.cloned.1.call-update) | async-done | bytes 5136
  319.8 1.1 copy.389
  320.9 28.0 %reduce-scatter.17.cloned.1.call-done = f32[640,2]{1,0:T(8,128)} async-done(((f32[2560,2]{1,0:T(8,128)}), f32[640,2]{1,0:T(8,128)}) %reduce-scatter.17.cloned.1.call-update) | async-done | bytes 5136
  348.9 1.1 copy.368
  350.0 28.0 %reduce-scatter.15.cloned.1.call-done = f32[640,2]{1,0:T(8,128)} async-done(((f32[2560,2]{1,0:T(8,128)}), f32[640,2]{1,0:T(8,128)}) %reduce-scatter.15.cloned.1.call-update) | async-done | bytes 5136
  378.0 1.1 copy.346
  379.1 27.8 %reduce-scatter.13.cloned.1.call-done = f32[640,2]{1,0:T(8,128)} async-done(((f32[2560,2]{1,0:T(8,128)}), f32[640,2]{1,0:T(8,128)}) %reduce-scatter.13.cloned.1.call-update) | async-done | bytes 5136
  406.9 1.1 copy.326
  408.2 0.6 copy.390
  (246 shorter events, 9.6 us)
Async XLA Ops:
  7.2 283.6 %copy-start = (bf16[512,2560]{1,0:T(8,128)(2,1)S(1)}, bf16[512,2560]{1,0:T(8,128)(2,1)}, u32[]{:S(2)}) copy-start(bf16[512,2560]{1,0:T(8,128)(2,1)} %param.25) | copy-start | bytes 7864324
  7.2 79.1 %copy-start.7 = (f32[2560]{0:T(1024)S(1)}, f32[2560]{0:T(1024)}, u32[]{:S(2)}) copy-start(f32[2560]{0:T(1024)} %param.19) | copy-start | bytes 30724
  7.2 79.1 %copy-start.5 = (bf16[2560,128]{1,0:T(8,128)(2,1)S(1)}, bf16[2560,128]{1,0:T(8,128)(2,1)}, u32[]{:S(2)}) copy-start(bf16[2560,128]{1,0:T(8,128)(2,1)} %param.24) | copy-start | bytes 1966084
  7.2 282.8 %all-reduce.4.cloned.1.call-start = ((), (), s32[]{:S(2)}) async-start(), calls=%async_computation.8 | async-start | bytes 278528 | tf_op jit(solution)/shard_map/psum | solution.py:152
  7.2 79.9 %copy-start.6 = (bf16[2560,128]{1,0:T(8,128)(2,1)S(1)}, bf16[2560,128]{1,0:T(8,128)(2,1)}, u32[]{:S(2)}) copy-start(bf16[2560,128]{1,0:T(8,128)(2,1)} %param.23) | copy-start | bytes 1966084
  8.5 47.0 %copy-start.16 = (bf16[1,2,640]{2,1,0:T(2,128)(2,1)}, bf16[1,2,640]{2,1,0:T(2,128)(2,1)S(1)}, u32[]{:S(2)}) copy-start(bf16[1,2,640]{2,1,0:T(2,128)(2,1)S(1)} %get-tuple-element.77) | copy-start | bytes 7684
  8.5 116.3 %copy-start.14 = (bf16[1,2,640]{2,1,0:T(2,128)(2,1)}, bf16[1,2,640]{2,1,0:T(2,128)(2,1)S(1)}, u32[]{:S(2)}) copy-start(bf16[1,2,640]{2,1,0:T(2,128)(2,1)S(1)} %get-tuple-element.78) | copy-start | bytes 7684
  8.5 117.7 %copy-start.18 = (bf16[1,2,640]{2,1,0:T(2,128)(2,1)}, bf16[1,2,640]{2,1,0:T(2,128)(2,1)S(1)}, u32[]{:S(2)}) copy-start(bf16[1,2,640]{2,1,0:T(2,128)(2,1)S(1)} %get-tuple-element.79) | copy-start | bytes 7684
  51.6 34.7 %copy-start.31 = (f32[16]{0:T(128)}, f32[16]{0:T(128)S(1)}, u32[]{:S(2)}) copy-start(f32[16]{0:T(128)S(1)} %add_rsqrt_fusion.11) | copy-start | bytes 196
  86.2 7.0 %copy-start.25 = (f32[16]{0:T(128)}, f32[16]{0:T(128)S(1)}, u32[]{:S(2)}) copy-start(f32[16]{0:T(128)S(1)} %add_rsqrt_fusion.7) | copy-start | bytes 196
  123.9 39.5 %copy-start.8 = (bf16[1,16,2560]{2,1,0:T(8,128)(2,1)}, bf16[1,16,2560]{2,1,0:T(8,128)(2,1)S(1)}, u32[]{:S(2)}) copy-start(bf16[1,16,2560]{2,1,0:T(8,128)(2,1)S(1)} %get-tuple-element.55) | copy-start | bytes 245764
  123.9 2.4 copy-start.27
  162.1 1.3 copy-start.10
  162.2 1.2 copy-start.29
  163.4 4.4 %copy-start.32 = (f32[16]{0:T(128)S(1)}, f32[16]{0:T(128)}, u32[]{:S(2)}) copy-start(f32[16]{0:T(128)} %copy-done.31) | copy-start | bytes 196
  167.8 2.8 copy-start.2
  167.8 2.8 copy-start.11
  167.8 2.8 copy-start.30
  167.8 3.7 copy-start.26
  170.6 1.9 copy-start.9
  170.6 1.9 copy-start.28
  171.5 2.0 copy-start.41
  171.6 2.0 copy-start.42
  171.6 2.0 copy-start.12
  171.6 2.0 copy-start.1
  171.6 2.7 copy-start.38
  171.6 2.7 copy-start.39
  171.6 2.7 copy-start.40
  171.6 2.8 copy-start.13
  171.6 2.8 copy-start.36
  171.7 2.9 copy-start.24
  171.7 3.5 copy-start.37
  172.6 2.8 copy-start.23
  172.6 3.7 copy-start.22
  172.6 4.5 %copy-start.21 = (bf16[16,128]{1,0:T(8,128)(2,1)S(1)}, bf16[16,128]{1,0:T(8,128)(2,1)}, u32[]{:S(2)}) copy-start(bf16[16,128]{1,0:T(8,128)(2,1)} %convolution_convert_fusion.2) | copy-start | bytes 12292
  172.6 5.4 %copy-start.20 = (bf16[16,128]{1,0:T(8,128)(2,1)S(1)}, bf16[16,128]{1,0:T(8,128)(2,1)}, u32[]{:S(2)}) copy-start(bf16[16,128]{1,0:T(8,128)(2,1)} %convolution_convert_fusion.3) | copy-start | bytes 12292
  178.7 5.0 %copy-start.3 = (bf16[16,256,128]{2,1,0:T(8,128)(2,1)S(1)}, bf16[16,256,128]{2,1,0:T(8,128)(2,1)}, u32[]{:S(2)}) copy-start(bf16[16,256,128]{2,1,0:T(8,128)(2,1)} %param.26) | copy-start | bytes 3145732
  187.9 5.0 %copy-start.4 = (bf16[16,256,128]{2,1,0:T(8,128)(2,1)S(1)}, bf16[16,256,128]{2,1,0:T(8,128)(2,1)}, u32[]{:S(2)}) copy-start(bf16[16,256,128]{2,1,0:T(8,128)(2,1)} %param.27) | copy-start | bytes 3145732
  220.9 98.8 %reduce-scatter.19.cloned.1.call-start = ((), (), s32[]{:S(2)}) async-start(), calls=%async_computation.7 | async-start | bytes 1638400
  290.8 3.2 copy-start.35
  293.7 3.3 copy-start.34
  293.7 55.1 %reduce-scatter.17.cloned.1.call-start = ((), (), s32[]{:S(2)}) async-start(), calls=%async_computation.6 | async-start | bytes 1638400
  297.1 3.1 copy-start.33
  297.1 80.9 %reduce-scatter.15.cloned.1.call-start = ((), (), s32[]{:S(2)}) async-start(), calls=%async_computation.5 | async-start | bytes 1638400
  300.3 106.7 %reduce-scatter.13.cloned.1.call-start = ((), (), s32[]{:S(2)}) async-start(), calls=%async_computation.4 | async-start | bytes 1638400
  300.3 107.7 %copy-start.17 = (bf16[1,2,640]{2,1,0:T(2,128)(2,1)S(1)}, bf16[1,2,640]{2,1,0:T(2,128)(2,1)}, u32[]{:S(2)}) copy-start(bf16[1,2,640]{2,1,0:T(2,128)(2,1)} %copy-done.16) | copy-start | bytes 7684
  300.3 107.7 %copy-start.19 = (bf16[1,2,640]{2,1,0:T(2,128)(2,1)S(1)}, bf16[1,2,640]{2,1,0:T(2,128)(2,1)}, u32[]{:S(2)}) copy-start(bf16[1,2,640]{2,1,0:T(2,128)(2,1)} %copy-done.18) | copy-start | bytes 7684
  300.4 107.7 %copy-start.15 = (bf16[1,2,640]{2,1,0:T(2,128)(2,1)S(1)}, bf16[1,2,640]{2,1,0:T(2,128)(2,1)}, u32[]{:S(2)}) copy-start(bf16[1,2,640]{2,1,0:T(2,128)(2,1)} %copy-done.14) | copy-start | bytes 7684
Sparse Core Ops, SparseCore 0:
  221.1 68.8 all-reduce.3
  293.9 25.8 reduce-scatter.18
  322.3 26.5 reduce-scatter.16
  351.4 26.5 reduce-scatter.14
  380.4 26.5 reduce-scatter.12
where the time goes:
time: 416 us; the launch traced here: 415 us
  blocking collectives  166 us (40%)
  waiting for transfers between devices  165 us (40%)
  matrix products  44.2 us (11%)
  local copies, waits for them, and re-layouts  19.6 us (5%)
  between operations  14.9 us (4%)
  other arithmetic  5.49 us (1%)
    all_gather x4, blocking collectives, shards(): portion = lax.all_gather(wide_states, 'seq', axis=1, tiled=True)  123 us
    unnamed x9, waiting for transfers between devices  99.2 us
    psum x1, waiting for transfers between devices, shards(): lax.psum((row_total * every_factor, row_mix * every_factor[..., None]), '...  65.4 us
    all_gather x4, blocking collectives, shards(): wide_states = lax.all_gather(block_states, 'mp', axis=2, tiled=True)  21.9 us
    pmax x1, blocking collectives, shards(): every_top = lax.pmax(row_top, 'seq')  21.5 us
    dot_general x4, matrix products, shards(): jnp.dot(attended, w_out, preferred_element_type=jnp.float32)  11.9 us
  transfers between devices with their start and end apart: 5, of which 5 were waited for; matrix products, arithmetic and copies ran while one was open for 4% of the time, Pallas kernels for 0%

commit v1 on v0

v1 whole, which is shorter than its diff:
```python
import functools
import math

import jax
import jax.numpy as jnp
from jax import lax
from jax.experimental import pallas as pl
from jax.experimental.pallas import tpu as pltpu
from jax.sharding import PartitionSpec as P

HEAD = 128
EPS = 1e-06
ROPE_BASE = 1000000.0
NEGATIVE = -1e30
F32 = jnp.float32
BF16 = jnp.bfloat16
MESH = pl.DeviceIdType.MESH
UNROLL_UP_TO = 8


def flip(index, k, n):
    total = 0
    bit = 1
    while bit < n:
        a = (index // bit) % 2
        b = (k // bit) % 2
        total = total + (a + b - 2 * a * b) * bit
        bit *= 2
    return total


def loop(low, high, body, carry):
    if high - low < UNROLL_UP_TO:
        for k in range(low, high):
            carry = body(k, carry)
        return carry
    return lax.fori_loop(low, high, body, carry)


def kernel(
    n_seq,
    n_mp,
    states,
    norm_gain,
    query_gain,
    key_gain,
    w_query,
    key_matrix,
    value_matrix,
    w_out,
    cached_keys,
    cached_values,
    req_len,
    slot_request,
    slot_block,
    slot_empty,
    hidden,
    new_keys,
    new_values,
    x_rows,
    x_parts,
    w_all,
    w_out_parts,
    k_all,
    v_all,
    q_rows,
    q_parts,
    o_out,
    o_in,
    st_out,
    st_in,
    att_rows,
    y_out,
    y_in,
    t_rows,
    first_slot,
    first_count,
    second_slot,
    second_count,
    load_sem,
    wo_sem,
    x_send,
    x_recv,
    q_send,
    q_recv,
    o_send,
    o_recv,
    st_send,
    st_recv,
    y_send,
    y_recv,
):
    steps, own, cols = states.shape
    rows = steps * own
    chunks = cols // HEAD
    width = cols * n_mp
    q_width = w_query.shape[1]
    heads = q_width // HEAD
    group = steps * heads
    slots, block_len, _ = cached_keys.shape
    requests = req_len.shape[0]
    scaling = HEAD**-0.5
    my_seq = lax.axis_index("seq")
    my_mp = lax.axis_index("mp")

    barrier = pltpu.get_barrier_semaphore()
    for k in range(1, n_mp):
        pl.semaphore_signal(
            barrier, inc=1, device_id={"mp": flip(my_mp, k, n_mp)}, device_id_type=MESH
        )

    def greet(k, carry):
        pl.semaphore_signal(
            barrier, inc=1, device_id={"seq": flip(my_seq, k, n_seq)}, device_id_type=MESH
        )
        return carry

    loop(1, n_seq, greet, 0)

    loads = [
        pltpu.make_async_copy(w_query, w_all.at[:, 0:q_width], load_sem.at[0]),
        pltpu.make_async_copy(key_matrix, w_all.at[:, q_width : q_width + HEAD], load_sem.at[1]),
        pltpu.make_async_copy(
            value_matrix, w_all.at[:, q_width + HEAD : q_width + 2 * HEAD], load_sem.at[2]
        ),
        pltpu.make_async_copy(cached_keys, k_all, load_sem.at[3]),
        pltpu.make_async_copy(cached_values, v_all, load_sem.at[4]),
    ]
    for k in range(n_mp):
        start = pl.multiple_of(flip(my_mp, k, n_mp) * cols, HEAD)
        loads.append(
            pltpu.make_async_copy(
                w_out.at[:, pl.ds(start, cols)], w_out_parts.at[k], wo_sem.at[k]
            )
        )
    for load in loads:
        load.start()

    for t in range(steps):
        block = states[t].astype(F32)
        for r in range(own):
            x_rows[r * steps + t : r * steps + t + 1, :] = block[r : r + 1, :]
    own_x = x_rows[...]
    pieces = [own_x[:, c * HEAD : (c + 1) * HEAD] for c in range(chunks)]
    padding = x_parts.shape[1] // rows - chunks
    pieces += [jnp.zeros((rows, HEAD), F32)] * padding
    x_parts[my_mp] = jnp.concatenate(pieces, axis=0).astype(BF16)

    pl.semaphore_wait(barrier, n_mp - 1 + n_seq - 1)

    x_copies = []
    for k in range(n_mp - 1, 0, -1):
        x_copies.append(
            pltpu.make_async_remote_copy(
                src_ref=x_parts.at[my_mp],
                dst_ref=x_parts.at[my_mp],
                send_sem=x_send.at[k],
                recv_sem=x_recv.at[k],
                device_id={"mp": flip(my_mp, k, n_mp)},
                device_id_type=MESH,
            )
        )
        x_copies[-1].start()

    owners = []
    for s in range(slots):
        request = slot_request[s]
        used = (slot_empty[s] == 0) & (slot_block[s] * block_len < req_len[request])
        owners.append(jnp.where(used, request, -1))

    def find(b, carry):
        last = jnp.int32(-1)
        earlier = jnp.int32(-1)
        for s in range(slots):
            match = owners[s] == b
            earlier = jnp.where(match, last, earlier)
            last = jnp.where(match, jnp.int32(s), last)
        for found, slot_ref, count_ref in (
            (last, first_slot, first_count),
            (earlier, second_slot, second_count),
        ):
            safe = jnp.maximum(found, 0)
            left = req_len[b] - slot_block[safe] * block_len
            slot_ref[b] = safe
            count_ref[b] = jnp.where(found >= 0, jnp.clip(left, 0, block_len), 0)
        return carry

    lax.fori_loop(0, requests, find, 0)

    row_id = lax.broadcasted_iota(jnp.int32, (rows, HEAD), 0)
    lane_id = lax.broadcasted_iota(jnp.int32, (rows, HEAD), 1)
    position = jnp.zeros((rows, HEAD), jnp.int32)
    for r in range(own):
        length = req_len[my_seq * own + r]
        position = jnp.where(row_id >= r * steps, length + row_id - r * steps, position)
    low_half = lane_id < HEAD // 2
    pair = jnp.where(low_half, lane_id, lane_id - HEAD // 2).astype(F32)
    frequency = jnp.exp(pair * (-2.0 * math.log(ROPE_BASE) / HEAD))
    angle = position.astype(F32) * frequency
    cosine = jnp.cos(angle)
    sine = jnp.sin(angle)
    sine = jnp.where(low_half, -sine, sine)

    def finish_head(values, gain):
        mean = jnp.mean(values * values, axis=-1, keepdims=True)
        values = values * lax.rsqrt(mean + EPS) * gain
        return values * cosine + pltpu.roll(values, HEAD // 2, 1) * sine

    for copy in x_copies:
        copy.wait_recv()
    blocks = []
    square = jnp.zeros((rows, HEAD), F32)
    for m in range(n_mp):
        part = x_parts[m].astype(F32)
        for c in range(chunks):
            piece = part[c * rows : (c + 1) * rows, :]
            blocks.append(piece)
            square = square + piece * piece
    mean = jnp.sum(square, axis=-1, keepdims=True) * (1.0 / width)
    factor = lax.rsqrt(mean + EPS)
    normed = (jnp.concatenate(blocks, axis=1) * factor * norm_gain[...]).astype(BF16)
    for load in loads[:3]:
        load.wait()
    projected = jnp.dot(normed, w_all[...], preferred_element_type=F32)

    for h in range(heads):
        one = finish_head(projected[:, h * HEAD : (h + 1) * HEAD], query_gain[...])
        for r in range(own):
            q_rows[r, h * steps : (h + 1) * steps, :] = one[r * steps : (r + 1) * steps, :]
    for r in range(own):
        q_parts[0, r] = q_rows[r].astype(BF16)

    def query_copy(k):
        return pltpu.make_async_remote_copy(
            src_ref=q_parts.at[0],
            dst_ref=q_parts.at[k],
            send_sem=q_send.at[k],
            recv_sem=q_recv.at[k],
            device_id={"seq": flip(my_seq, k, n_seq)},
            device_id_type=MESH,
        )

    def send_query(i, carry):
        query_copy(n_seq - i).start()
        return carry

    loop(1, n_seq, send_query, 0)

    own_keys = finish_head(projected[:, q_width : q_width + HEAD], key_gain[...])
    own_values = projected[:, q_width + HEAD : q_width + 2 * HEAD]
    for source, target in ((own_keys, new_keys), (own_values, new_values)):
        for r in range(own):
            for t in range(steps):
                t_rows[t * own + r : t * own + r + 1, 0:HEAD] = source[
                    r * steps + t : r * steps + t + 1, :
                ]
        for t in range(steps):
            target[t] = t_rows[t * own : (t + 1) * own, 0:HEAD].astype(BF16)
    own_keys = own_keys.astype(BF16)
    own_values = own_values.astype(BF16)

    for load in loads[3:5]:
        load.wait()

    key_lane = lax.broadcasted_iota(jnp.int32, (group, block_len), 1)
    contract = (((1,), (1,)), ((), ()))

    def masked_scores(query, slot, count):
        scores = lax.dot_general(query, k_all[slot], contract, preferred_element_type=F32)
        return jnp.where(key_lane < count, scores * scaling, NEGATIVE)

    def masked_weights(scores, top, count):
        return jnp.where(key_lane < count, jnp.exp(scores - top), 0.0)

    def row_max(values):
        return jnp.max(values, axis=-1, keepdims=True)

    def row_sum(values):
        return jnp.sum(values, axis=-1, keepdims=True)

    fresh_col = lax.broadcasted_iota(jnp.int32, (group, rows), 1)
    fresh_row = lax.broadcasted_iota(jnp.int32, (group, rows), 0) % steps
    state = []
    for r in range(own):
        b = my_seq * own + r
        query = q_parts[0, r]
        one, one_count = first_slot[b], first_count[b]
        two, two_count = second_slot[b], second_count[b]
        score_one = masked_scores(query, one, one_count)
        score_two = masked_scores(query, two, two_count)
        allowed = (fresh_col >= r * steps) & (fresh_col - r * steps <= fresh_row)
        fresh = lax.dot_general(query, own_keys, contract, preferred_element_type=F32)
        fresh = jnp.where(allowed, fresh * scaling, NEGATIVE)
        top = jnp.maximum(jnp.maximum(row_max(score_one), row_max(score_two)), row_max(fresh))
        weight_one = masked_weights(score_one, top, one_count)
        weight_two = masked_weights(score_two, top, two_count)
        weight_new = jnp.where(allowed, jnp.exp(fresh - top), 0.0)
        total = row_sum(weight_one + weight_two) + row_sum(weight_new)
        mix = (
            jnp.dot(weight_one.astype(BF16), v_all[one], preferred_element_type=F32)
            + jnp.dot(weight_two.astype(BF16), v_all[two], preferred_element_type=F32)
            + jnp.dot(weight_new.astype(BF16), own_values, preferred_element_type=F32)
        )
        state += [top, total, mix]

    stat_lane = lax.broadcasted_iota(jnp.int32, (group, HEAD), 1)
    stat_row = lax.broadcasted_iota(jnp.int32, (group, HEAD), 0)
    at_top = stat_lane == stat_row
    at_total = stat_lane == stat_row + HEAD // 2
    stat_rows = st_out.shape[1]

    def partial_copies(k):
        there = {"seq": flip(my_seq, k, n_seq)}
        return (
            pltpu.make_async_remote_copy(
                src_ref=o_out.at[k],
                dst_ref=o_in.at[k],
                send_sem=o_send.at[k],
                recv_sem=o_recv.at[k],
                device_id=there,
                device_id_type=MESH,
            ),
            pltpu.make_async_remote_copy(
                src_ref=st_out.at[k],
                dst_ref=st_in.at[k],
                send_sem=st_send.at[k],
                recv_sem=st_recv.at[k],
                device_id=there,
                device_id_type=MESH,
            ),
        )

    def serve(k, carry):
        query_copy(k).wait_recv()
        peer = flip(my_seq, k, n_seq)
        lines = []
        for r in range(own):
            b = peer * own + r
            slot, count = first_slot[b], first_count[b]
            scores = masked_scores(q_parts[k, r], slot, count)
            top = row_max(scores)
            weights = masked_weights(scores, top, count)
            total = row_sum(weights)
            mix = jnp.dot(weights.astype(BF16), v_all[slot], preferred_element_type=F32)
            o_out[k, r] = mix.astype(BF16)
            spread = jnp.where(at_top, top, jnp.where(at_total, total, 0.0))
            lines.append(jnp.sum(spread, axis=0, keepdims=True))
        lines.append(jnp.zeros((stat_rows - own, HEAD), F32))
        st_out[k] = jnp.concatenate(lines, axis=0)
        for copy in partial_copies(k):
            copy.start()
        return carry

    loop(1, n_seq, serve, 0)

    def merge(k, carry):
        for copy in partial_copies(k):
            copy.wait_recv()
        carry = list(carry)
        for r in range(own):
            top, total, mix = carry[3 * r : 3 * r + 3]
            line = jnp.broadcast_to(st_in[k, r : r + 1, :], (group, HEAD))
            their_top = row_sum(jnp.where(at_top, line, 0.0))
            their_total = row_sum(jnp.where(at_total, line, 0.0))
            overall = jnp.maximum(top, their_top)
            ours = jnp.exp(top - overall)
            theirs = jnp.exp(their_top - overall)
            carry[3 * r] = overall
            carry[3 * r + 1] = total * ours + their_total * theirs
            carry[3 * r + 2] = mix * ours + o_in[k, r].astype(F32) * theirs
        return tuple(carry)

    state = loop(1, n_seq, merge, tuple(state))

    for r in range(own):
        attended = state[3 * r + 2] / state[3 * r + 1]
        for h in range(heads):
            att_rows[r * steps : (r + 1) * steps, h * HEAD : (h + 1) * HEAD] = attended[
                h * steps : (h + 1) * steps, :
            ]
    attended = att_rows[...].astype(BF16)

    y_copies = []
    for k in range(n_mp - 1, 0, -1):
        loads[5 + k].wait()
        y_out[k] = jnp.dot(attended, w_out_parts[k], preferred_element_type=F32)
        y_copies.append(
            pltpu.make_async_remote_copy(
                src_ref=y_out.at[k],
                dst_ref=y_in.at[k],
                send_sem=y_send.at[k],
                recv_sem=y_recv.at[k],
                device_id={"mp": flip(my_mp, k, n_mp)},
                device_id_type=MESH,
            )
        )
        y_copies[-1].start()
    loads[5].wait()
    summed = jnp.dot(attended, w_out_parts[0], preferred_element_type=F32)
    for copy in y_copies:
        copy.wait_recv()
    for k in range(1, n_mp):
        summed = summed + y_in[k]
    result = x_rows[...] + summed
    for r in range(own):
        for t in range(steps):
            t_rows[t * own + r : t * own + r + 1, :] = result[
                r * steps + t : r * steps + t + 1, :
            ]
    for t in range(steps):
        hidden[t] = t_rows[t * own : (t + 1) * own, :].astype(BF16)

    for copy in x_copies + y_copies:
        copy.wait_send()

    def drain(k, carry):
        query_copy(k).wait_send()
        for copy in partial_copies(k):
            copy.wait_send()
        return carry

    loop(1, n_seq, drain, 0)


def shards(n_seq, n_mp, *args):
    (
        states,
        norm_gain,
        query_gain,
        key_gain,
        w_query,
        key_matrix,
        value_matrix,
        w_out,
        cached_keys,
        cached_values,
        req_len,
        slot_request,
        slot_block,
        slot_empty,
    ) = args
    steps, own, cols = states.shape
    width, q_width = w_query.shape
    heads = q_width // HEAD
    group = steps * heads
    rows = steps * own
    slots, block_len, _ = cached_keys.shape
    requests = req_len.shape[0]
    assert key_matrix.shape[1] == HEAD
    part_rows = -(-(rows * (cols // HEAD)) // 16) * 16
    stat_rows = -(-own // 8) * 8
    vmem = pl.BlockSpec(memory_space=pltpu.VMEM)
    smem = pl.BlockSpec(memory_space=pltpu.SMEM)
    far = pl.BlockSpec(memory_space=pl.ANY)
    dma = pltpu.SemaphoreType.DMA
    return pl.pallas_call(
        functools.partial(kernel, n_seq, n_mp),
        out_shape=(
            jax.ShapeDtypeStruct(states.shape, BF16),
            jax.ShapeDtypeStruct((steps, own, HEAD), BF16),
            jax.ShapeDtypeStruct((steps, own, HEAD), BF16),
        ),
        in_specs=[vmem] * 4 + [far] * 6 + [smem] * 4,
        out_specs=(vmem, vmem, vmem),
        scratch_shapes=[
            pltpu.VMEM((rows, cols), F32),
            pltpu.VMEM((n_mp, part_rows, HEAD), BF16),
            pltpu.VMEM((width, q_width + 2 * HEAD), BF16),
            pltpu.VMEM((n_mp, q_width, cols), BF16),
            pltpu.VMEM((slots, block_len, HEAD), BF16),
            pltpu.VMEM((slots, block_len, HEAD), BF16),
            pltpu.VMEM((own, group, HEAD), F32),
            pltpu.VMEM((n_seq, own, group, HEAD), BF16),
            pltpu.VMEM((n_seq, own, group, HEAD), BF16),
            pltpu.VMEM((n_seq, own, group, HEAD), BF16),
            pltpu.VMEM((n_seq, stat_rows, HEAD), F32),
            pltpu.VMEM((n_seq, stat_rows, HEAD), F32),
            pltpu.VMEM((rows, q_width), F32),
            pltpu.VMEM((n_mp, rows, cols), F32),
            pltpu.VMEM((n_mp, rows, cols), F32),
            pltpu.VMEM((rows, cols), F32),
            pltpu.SMEM((requests,), jnp.int32),
            pltpu.SMEM((requests,), jnp.int32),
            pltpu.SMEM((requests,), jnp.int32),
            pltpu.SMEM((requests,), jnp.int32),
            dma((5,)),
            dma((n_mp,)),
            dma((n_mp,)),
            dma((n_mp,)),
            dma((n_seq,)),
            dma((n_seq,)),
            dma((n_seq,)),
            dma((n_seq,)),
            dma((n_seq,)),
            dma((n_seq,)),
            dma((n_mp,)),
            dma((n_mp,)),
        ],
        compiler_params=pltpu.CompilerParams(
            collective_id=0, has_side_effects=True, vmem_limit_bytes=48 * 1024 * 1024
        ),
    )(
        states,
        norm_gain.reshape(1, -1),
        query_gain.reshape(1, -1),
        key_gain.reshape(1, -1),
        w_query,
        key_matrix,
        value_matrix,
        w_out,
        cached_keys,
        cached_values,
        req_len,
        slot_request,
        slot_block,
        slot_empty,
    )


def solution(mesh):
    placed = (
        P(None, "seq", "mp"),
        P(),
        P(),
        P(),
        P(None, "mp"),
        P(None, "mp"),
        P(None, "mp"),
        P("mp", None),
        P("seq", None, "mp"),
        P("seq", None, "mp"),
        P(),
        P("seq"),
        P("seq"),
        P("seq"),
    )
    return jax.shard_map(
        functools.partial(shards, mesh.shape["seq"], mesh.shape["mp"]),
        mesh=mesh,
        in_specs=placed,
        out_specs=(P(None, "seq", "mp"), P(None, "seq", "mp"), P(None, "seq", "mp")),
        check_vma=False,
    )
```

time: 416 us -> 38.5 us (0.09)
  blocking collectives: 166 us -> 0 us
  waiting for transfers between devices: 165 us -> 0 us
  matrix products: 44.2 us -> 0 us
  Pallas kernels: 0 us -> 23.9 us
  between operations: 14.9 us -> 0.65 us
  local copies, waits for them, and re-layouts: 19.6 us -> 13.5 us
  other arithmetic: 5.49 us -> 0 us
    all_gather x8 -> x0, blocking collectives: 145 us -> none  [the longest x4 123 us: shards(): portion = lax.all_gather(wide_states, 'seq', axis=1, tiled=True)]
    unnamed x9 -> x0, waiting for transfers between devices: 99.2 us -> none
    psum x1 -> x0, waiting for transfers between devices: 65.4 us -> none  [shards(): lax.psum((row_total * every_factor, row_mix * every_factor[..., None]), '...]
    dot_general x39 -> x0, matrix products: 44.2 us -> none  [the longest x4 11.9 us: shards(): jnp.dot(attended, w_out, preferred_element_type=jnp.float32)]
    pallas_call x0 -> x1, Pallas kernels: none -> 23.9 us  [shards(): pl.pallas_call(functools.partial(kernel, n_seq, n_mp), out_shape=(jax.Sha...]
    pmax x1 -> x0, blocking collectives: 21.5 us -> none  [shards(): every_top = lax.pmax(row_top, 'seq')]
    unnamed x100 -> x27, local copies, waits for them, and re-layouts: 2.05 us -> 12.7 us
    gather x13 -> x0, local copies, waits for them, and re-layouts: 5.59 us -> none  [the longest x8 2.58 us: shards(): slot_reference = jnp.take(row_top, slot_request, axis=1)]
  transfers between devices with their start and end apart: 5 -> 0, of which waited for: 5 -> 0; matrix products, arithmetic and copies ran while one was open for 4% -> 0% of each run, Pallas kernels for 0% -> 0%
where the time goes in v1:
time: 38.5 us; the launch traced here: 38 us
  Pallas kernels  23.9 us (62%)
  local copies, waits for them, and re-layouts  13.5 us (35%)
  between operations  0.65 us (2%)
    pallas_call x1, Pallas kernels, shards(): pl.pallas_call(functools.partial(kernel, n_seq, n_mp), out_shape=(jax.Sha...  23.9 us
    unnamed x27, local copies, waits for them, and re-layouts  12.7 us

profile of v1, /device:TPU:0, one launch (start us, length us, event | category | flops | bytes accessed | tf_op | source)
XLA Modules:
  0.0 38.0 jit_solution(13858009636775186204)
XLA Ops:
  0.6 0.7 %reshape.15.norm_gain = f32[1,2560]{1,0:T(1,128)S(1)} reshape(f32[2560]{0:T(1024)} %param.15) | data formatting | bytes 20480 | tf_op jit(solution)/shard_map/reshape | solution.py:504
  1.3 0.0 copy-start
  1.4 1.7 %copy-done = bf16[2560,512]{1,0:T(8,128)(2,1)S(1)} copy-done((bf16[2560,512]{1,0:T(8,128)(2,1)S(1)}, bf16[2560,512]{1,0:T(8,128)(2,1)}, u32[]{:S(2)}) %copy-start) | copy-done | bytes 2621464
  3.1 0.0 copy-start.1
  3.1 1.2 %copy-done.1 = bf16[16,256,128]{2,1,0:T(8,128)(2,1)S(1)} copy-done((bf16[16,256,128]{2,1,0:T(8,128)(2,1)S(1)}, bf16[16,256,128]{2,1,0:T(8,128)(2,1)}, u32[]{:S(2)}) %copy-start.1) | copy-done | bytes 1048600
  4.3 0.0 copy-start.2
  4.3 1.2 %copy-done.2 = bf16[16,256,128]{2,1,0:T(8,128)(2,1)S(1)} copy-done((bf16[16,256,128]{2,1,0:T(8,128)(2,1)S(1)}, bf16[16,256,128]{2,1,0:T(8,128)(2,1)}, u32[]{:S(2)}) %copy-start.2) | copy-done | bytes 1048600
  5.5 0.0 copy-start.3
  5.5 1.1 %copy-done.3 = bf16[2560,128]{1,0:T(8,128)(2,1)S(1)} copy-done((bf16[2560,128]{1,0:T(8,128)(2,1)S(1)}, bf16[2560,128]{1,0:T(8,128)(2,1)}, u32[]{:S(2)}) %copy-start.3) | copy-done | bytes 655384
  6.6 0.0 copy-start.4
  6.6 1.1 %copy-done.4 = bf16[2560,128]{1,0:T(8,128)(2,1)S(1)} copy-done((bf16[2560,128]{1,0:T(8,128)(2,1)S(1)}, bf16[2560,128]{1,0:T(8,128)(2,1)}, u32[]{:S(2)}) %copy-start.4) | copy-done | bytes 655384
  7.7 0.0 copy-start.5
  7.7 0.7 %copy-done.5 = bf16[4,2,640]{2,1,0:T(2,128)(2,1)S(1)} copy-done((bf16[4,2,640]{2,1,0:T(2,128)(2,1)S(1)}, bf16[4,2,640]{2,1,0:T(2,128)(2,1)}, u32[]{:S(2)}) %copy-start.5) | copy-done | bytes 10264
  8.4 0.0 copy-start.6
  8.4 0.7 %copy-done.6 = f32[128]{0:T(128)S(1)} copy-done((f32[128]{0:T(128)S(1)}, f32[128]{0:T(128)}, u32[]{:S(2)}) %copy-start.6) | copy-done | bytes 536
  9.1 0.0 copy-start.7
  9.1 0.7 %copy-done.7 = f32[128]{0:T(128)S(1)} copy-done((f32[128]{0:T(128)S(1)}, f32[128]{0:T(128)}, u32[]{:S(2)}) %copy-start.7) | copy-done | bytes 536
  9.7 0.0 copy-start.8
  9.7 0.7 %copy-done.8 = s32[16]{0:T(128)S(1)} copy-done((s32[16]{0:T(128)S(1)}, s32[16]{0:T(128)}, u32[]{:S(2)}) %copy-start.8) | copy-done | bytes 88
  10.4 0.0 copy-start.9
  10.4 0.7 %copy-done.9 = s32[16]{0:T(128)S(1)} copy-done((s32[16]{0:T(128)S(1)}, s32[16]{0:T(128)}, u32[]{:S(2)}) %copy-start.9) | copy-done | bytes 88
  11.0 0.0 copy-start.10
  11.0 0.7 %copy-done.10 = s32[16]{0:T(128)S(1)} copy-done((s32[16]{0:T(128)S(1)}, s32[16]{0:T(128)}, u32[]{:S(2)}) %copy-start.10) | copy-done | bytes 88
  11.7 0.0 copy-start.11
  11.7 0.7 %copy-done.11 = s32[16]{0:T(128)S(1)} copy-done((s32[16]{0:T(128)S(1)}, s32[16]{0:T(128)}, u32[]{:S(2)}) %copy-start.11) | copy-done | bytes 88
  12.3 23.9 %shard_map.157 = (bf16[4,2,640]{2,1,0:T(2,128)(2,1)S(1)}, bf16[4,2,128]{2,1,0:T(2,128)(2,1)S(1)}, bf16[4,2,128]{2,1,0:T(2,128)(2,1)S(1)}) custom-call(bf16[4,2,640]{2,1,0:T(2,128)(2,1)S(1)} %copy-done.5, f32[1,2560]{1,0:T(1,128)S(1)} %reshape.15.norm_gain, f32[1,128]{1,0:T(1,128)S(1)} %bitcast.2, f32[1,128]{1,0:T(1,128)S(1)} %bitcast.3, ...), custom_call_target="tpu_custom_call" | custom-call | tf_op jit(solution)/shard_map/pallas_call | solution.py:456
  36.3 0.6 %copy.20 = bf16[4,2,640]{2,1,0:T(2,128)(2,1)} copy(bf16[4,2,640]{2,1,0:T(2,128)(2,1)S(1)} %get-tuple-element.6) | data formatting | bytes 20480
  36.9 0.6 %copy.21 = bf16[4,2,128]{2,1,0:T(2,128)(2,1)} copy(bf16[4,2,128]{2,1,0:T(2,128)(2,1)S(1)} %get-tuple-element.7) | data formatting | bytes 4096
  37.5 0.6 %copy.22 = bf16[4,2,128]{2,1,0:T(2,128)(2,1)} copy(bf16[4,2,128]{2,1,0:T(2,128)(2,1)S(1)} %get-tuple-element.8) | data formatting | bytes 4096
Async XLA Ops:
  1.3 1.7 %copy-start = (bf16[2560,512]{1,0:T(8,128)(2,1)S(1)}, bf16[2560,512]{1,0:T(8,128)(2,1)}, u32[]{:S(2)}) copy-start(bf16[2560,512]{1,0:T(8,128)(2,1)} %w_query.1) | copy-start | bytes 7864324
  3.1 1.2 %copy-start.1 = (bf16[16,256,128]{2,1,0:T(8,128)(2,1)S(1)}, bf16[16,256,128]{2,1,0:T(8,128)(2,1)}, u32[]{:S(2)}) copy-start(bf16[16,256,128]{2,1,0:T(8,128)(2,1)} %cached_keys.1) | copy-start | bytes 3145732
  4.3 1.2 %copy-start.2 = (bf16[16,256,128]{2,1,0:T(8,128)(2,1)S(1)}, bf16[16,256,128]{2,1,0:T(8,128)(2,1)}, u32[]{:S(2)}) copy-start(bf16[16,256,128]{2,1,0:T(8,128)(2,1)} %cached_values.1) | copy-start | bytes 3145732
  5.5 1.1 %copy-start.3 = (bf16[2560,128]{1,0:T(8,128)(2,1)S(1)}, bf16[2560,128]{1,0:T(8,128)(2,1)}, u32[]{:S(2)}) copy-start(bf16[2560,128]{1,0:T(8,128)(2,1)} %key_matrix.1) | copy-start | bytes 1966084
  6.6 1.1 %copy-start.4 = (bf16[2560,128]{1,0:T(8,128)(2,1)S(1)}, bf16[2560,128]{1,0:T(8,128)(2,1)}, u32[]{:S(2)}) copy-start(bf16[2560,128]{1,0:T(8,128)(2,1)} %value_matrix.1) | copy-start | bytes 1966084
  7.7 0.7 %copy-start.5 = (bf16[4,2,640]{2,1,0:T(2,128)(2,1)S(1)}, bf16[4,2,640]{2,1,0:T(2,128)(2,1)}, u32[]{:S(2)}) copy-start(bf16[4,2,640]{2,1,0:T(2,128)(2,1)} %states.1) | copy-start | bytes 30724
  8.4 0.7 %copy-start.6 = (f32[128]{0:T(128)S(1)}, f32[128]{0:T(128)}, u32[]{:S(2)}) copy-start(f32[128]{0:T(128)} %param.16) | copy-start | bytes 1540
  9.1 0.7 %copy-start.7 = (f32[128]{0:T(128)S(1)}, f32[128]{0:T(128)}, u32[]{:S(2)}) copy-start(f32[128]{0:T(128)} %param.17) | copy-start | bytes 1540
  9.7 0.7 %copy-start.8 = (s32[16]{0:T(128)S(1)}, s32[16]{0:T(128)}, u32[]{:S(2)}) copy-start(s32[16]{0:T(128)} %req_len.1) | copy-start | bytes 196
  10.4 0.7 %copy-start.9 = (s32[16]{0:T(128)S(1)}, s32[16]{0:T(128)}, u32[]{:S(2)}) copy-start(s32[16]{0:T(128)} %slot_request.1) | copy-start | bytes 196
  11.0 0.7 %copy-start.10 = (s32[16]{0:T(128)S(1)}, s32[16]{0:T(128)}, u32[]{:S(2)}) copy-start(s32[16]{0:T(128)} %slot_block.1) | copy-start | bytes 196
  11.7 0.7 %copy-start.11 = (s32[16]{0:T(128)S(1)}, s32[16]{0:T(128)}, u32[]{:S(2)}) copy-start(s32[16]{0:T(128)} %slot_empty.1) | copy-start | bytes 196

commit v2 on v1

--- a/solution.py
+++ b/solution.py
@@ -40,23 +40,31 @@
 def kernel(
     n_seq,
     n_mp,
-    states,
-    norm_gain,
-    query_gain,
-    key_gain,
+    states_far,
+    norm_gain_far,
+    query_gain_far,
+    key_gain_far,
     w_query,
     key_matrix,
     value_matrix,
     w_out,
     cached_keys,
     cached_values,
+    req_len_far,
+    slot_request_far,
+    slot_block_far,
+    slot_empty_far,
+    hidden,
+    new_keys,
+    new_values,
+    states,
+    norm_gain,
+    query_gain,
+    key_gain,
     req_len,
     slot_request,
     slot_block,
     slot_empty,
-    hidden,
-    new_keys,
-    new_values,
     x_rows,
     x_parts,
     w_all,
@@ -77,6 +85,7 @@
     first_count,
     second_slot,
     second_count,
+    small_sem,
     load_sem,
     wo_sem,
     x_send,
@@ -103,6 +112,24 @@
     my_seq = lax.axis_index("seq")
     my_mp = lax.axis_index("mp")
 
+    smalls = [
+        pltpu.make_async_copy(source, target, small_sem.at[i])
+        for i, (source, target) in enumerate(
+            (
+                (states_far, states),
+                (req_len_far, req_len),
+                (slot_request_far, slot_request),
+                (slot_block_far, slot_block),
+                (slot_empty_far, slot_empty),
+                (norm_gain_far, norm_gain),
+                (query_gain_far, query_gain),
+                (key_gain_far, key_gain),
+            )
+        )
+    ]
+    for small in smalls:
+        small.start()
+
     barrier = pltpu.get_barrier_semaphore()
     for k in range(1, n_mp):
         pl.semaphore_signal(
@@ -136,6 +163,7 @@
     for load in loads:
         load.start()
 
+    smalls[0].wait()
     for t in range(steps):
         block = states[t].astype(F32)
         for r in range(own):
@@ -161,6 +189,9 @@
             )
         )
         x_copies[-1].start()
+
+    for small in smalls[1:]:
+        small.wait()
 
     owners = []
     for s in range(slots):
@@ -218,7 +249,10 @@
             square = square + piece * piece
     mean = jnp.sum(square, axis=-1, keepdims=True) * (1.0 / width)
     factor = lax.rsqrt(mean + EPS)
-    normed = (jnp.concatenate(blocks, axis=1) * factor * norm_gain[...]).astype(BF16)
+    gains = norm_gain[...]
+    normed = jnp.concatenate(
+        [piece * factor * gains[i : i + 1, :] for i, piece in enumerate(blocks)], axis=1
+    ).astype(BF16)
     for load in loads[:3]:
         load.wait()
     projected = jnp.dot(normed, w_all[...], preferred_element_type=F32)
@@ -330,47 +364,68 @@
             ),
         )
 
-    def serve(k, carry):
-        query_copy(k).wait_recv()
-        peer = flip(my_seq, k, n_seq)
+    def serve(ks):
+        jobs = []
+        for k in ks:
+            query_copy(k).wait_recv()
+        for k in ks:
+            peer = flip(my_seq, k, n_seq)
+            for r in range(own):
+                b = peer * own + r
+                jobs.append((k, r, first_slot[b], first_count[b]))
+        scores = [masked_scores(q_parts[k, r], slot, count) for k, r, slot, count in jobs]
+        tops = [row_max(score) for score in scores]
+        weights = [
+            masked_weights(score, top, job[3]) for score, top, job in zip(scores, tops, jobs)
+        ]
+        totals = [row_sum(weight) for weight in weights]
         lines = []
-        for r in range(own):
-            b = peer * own + r
-            slot, count = first_slot[b], first_count[b]
-            scores = masked_scores(q_parts[k, r], slot, count)
-            top = row_max(scores)
-            weights = masked_weights(scores, top, count)
-            total = row_sum(weights)
-            mix = jnp.dot(weights.astype(BF16), v_all[slot], preferred_element_type=F32)
+        for (k, r, slot, _), weight, top, total in zip(jobs, weights, tops, totals):
+            mix = jnp.dot(weight.astype(BF16), v_all[slot], preferred_element_type=F32)
             o_out[k, r] = mix.astype(BF16)
             spread = jnp.where(at_top, top, jnp.where(at_total, total, 0.0))
             lines.append(jnp.sum(spread, axis=0, keepdims=True))
-        lines.append(jnp.zeros((stat_rows - own, HEAD), F32))
-        st_out[k] = jnp.concatenate(lines, axis=0)
-        for copy in partial_copies(k):
-            copy.start()
-        return carry
-
-    loop(1, n_seq, serve, 0)
-
-    def merge(k, carry):
-        for copy in partial_copies(k):
-            copy.wait_recv()
+        blank = jnp.zeros((stat_rows - own, HEAD), F32)
+        for i, k in enumerate(ks):
+            st_out[k] = jnp.concatenate(lines[i * own : (i + 1) * own] + [blank], axis=0)
+        for k in ks:
+            for copy in partial_copies(k):
+                copy.start()
+
+    def merge(ks, carry):
+        for k in ks:
+            for copy in partial_copies(k):
+                copy.wait_recv()
         carry = list(carry)
         for r in range(own):
-            top, total, mix = carry[3 * r : 3 * r + 3]
-            line = jnp.broadcast_to(st_in[k, r : r + 1, :], (group, HEAD))
-            their_top = row_sum(jnp.where(at_top, line, 0.0))
-            their_total = row_sum(jnp.where(at_total, line, 0.0))
-            overall = jnp.maximum(top, their_top)
-            ours = jnp.exp(top - overall)
-            theirs = jnp.exp(their_top - overall)
+            tops, totals, mixes = ([item] for item in carry[3 * r : 3 * r + 3])
+            for k in ks:
+                line = jnp.broadcast_to(st_in[k, r : r + 1, :], (group, HEAD))
+                tops.append(row_sum(jnp.where(at_top, line, 0.0)))
+                totals.append(row_sum(jnp.where(at_total, line, 0.0)))
+                mixes.append(o_in[k, r].astype(F32))
+            overall = functools.reduce(jnp.maximum, tops)
+            factors = [jnp.exp(top - overall) for top in tops]
             carry[3 * r] = overall
-            carry[3 * r + 1] = total * ours + their_total * theirs
-            carry[3 * r + 2] = mix * ours + o_in[k, r].astype(F32) * theirs
+            carry[3 * r + 1] = sum(total * f for total, f in zip(totals, factors))
+            carry[3 * r + 2] = sum(mix * f for mix, f in zip(mixes, factors))
         return tuple(carry)
 
-    state = loop(1, n_seq, merge, tuple(state))
+    state = tuple(state)
+    if n_seq <= UNROLL_UP_TO:
+        groups = [range(1, n_seq // 2), range(n_seq // 2, n_seq)]
+        for ks in groups:
+            serve(ks)
+        for ks in groups:
+            state = merge(ks, state)
+    else:
+
+        def serve_one(k, carry):
+            serve([k])
+            return carry
+
+        lax.fori_loop(1, n_seq, serve_one, 0)
+        state = lax.fori_loop(1, n_seq, lambda k, carry: merge([k], carry), state)
 
     for r in range(own):
         attended = state[3 * r + 2] / state[3 * r + 1]
@@ -450,8 +505,7 @@
     part_rows = -(-(rows * (cols // HEAD)) // 16) * 16
     stat_rows = -(-own // 8) * 8
     vmem = pl.BlockSpec(memory_space=pltpu.VMEM)
-    smem = pl.BlockSpec(memory_space=pltpu.SMEM)
-    far = pl.BlockSpec(memory_space=pl.ANY)
+    far = pl.BlockSpec(memory_space=pltpu.HBM)
     dma = pltpu.SemaphoreType.DMA
     return pl.pallas_call(
         functools.partial(kernel, n_seq, n_mp),
@@ -460,9 +514,17 @@
             jax.ShapeDtypeStruct((steps, own, HEAD), BF16),
             jax.ShapeDtypeStruct((steps, own, HEAD), BF16),
         ),
-        in_specs=[vmem] * 4 + [far] * 6 + [smem] * 4,
+        in_specs=[far] * 14,
         out_specs=(vmem, vmem, vmem),
         scratch_shapes=[
+            pltpu.VMEM(states.shape, BF16),
+            pltpu.VMEM((width // HEAD, HEAD), F32),
+            pltpu.VMEM((1, HEAD), F32),
+            pltpu.VMEM((1, HEAD), F32),
+            pltpu.SMEM((requests,), jnp.int32),
+            pltpu.SMEM((slots,), jnp.int32),
+            pltpu.SMEM((slots,), jnp.int32),
+            pltpu.SMEM((slots,), jnp.int32),
             pltpu.VMEM((rows, cols), F32),
             pltpu.VMEM((n_mp, part_rows, HEAD), BF16),
             pltpu.VMEM((width, q_width + 2 * HEAD), BF16),
@@ -483,6 +545,7 @@
             pltpu.SMEM((requests,), jnp.int32),
             pltpu.SMEM((requests,), jnp.int32),
             pltpu.SMEM((requests,), jnp.int32),
+            dma((8,)),
             dma((5,)),
             dma((n_mp,)),
             dma((n_mp,)),
@@ -497,11 +560,11 @@
             dma((n_mp,)),
         ],
         compiler_params=pltpu.CompilerParams(
-            collective_id=0, has_side_effects=True, vmem_limit_bytes=48 * 1024 * 1024
+            collective_id=0, has_side_effects=True, vmem_limit_bytes=63 * 1024 * 1024
         ),
     )(
         states,
-        norm_gain.reshape(1, -1),
+        norm_gain.reshape(-1, HEAD),
         query_gain.reshape(1, -1),
         key_gain.reshape(1, -1),
         w_query,

time: 38.5 us -> 28.2 us (0.73)
  local copies, waits for them, and re-layouts: 13.5 us -> 3.79 us
  Pallas kernels: 23.9 us -> 23.5 us
    unnamed x27 -> x3, local copies, waits for them, and re-layouts: 12.7 us -> 3.79 us
    reshape x1 -> x0, local copies, waits for them, and re-layouts: 0.72 us -> none  [shards(): norm_gain.reshape(1, -1)]
    pallas_call x1, Pallas kernels: 23.9 us -> 23.5 us  [shards(): pl.pallas_call(functools.partial(kernel, n_seq, n_mp), out_shape=(jax.Sha...]
where the time goes in v2:
time: 28.2 us; the launch traced here: 27.9 us
  Pallas kernels  23.5 us (83%)
  local copies, waits for them, and re-layouts  3.79 us (13%)
  between operations  0.65 us (2%)
    pallas_call x1, Pallas kernels, shards(): pl.pallas_call(functools.partial(kernel, n_seq, n_mp), out_shape=(jax.Sha...  23.5 us
    unnamed x3, local copies, waits for them, and re-layouts  3.79 us

profile of v2, /device:TPU:0, one launch (start us, length us, event | category | flops | bytes accessed | tf_op | source)
XLA Modules:
  0.0 27.9 jit_solution(8469676017285436009)
XLA Ops:
  0.6 23.5 %shard_map.157 = (bf16[4,2,640]{2,1,0:T(2,128)(2,1)}, bf16[4,2,128]{2,1,0:T(2,128)(2,1)}, bf16[4,2,128]{2,1,0:T(2,128)(2,1)}) custom-call(bf16[4,2,640]{2,1,0:T(2,128)(2,1)} %states_far.1, f32[20,128]{1,0:T(8,128)} %bitcast.3, f32[1,128]{1,0:T(1,128)} %bitcast.4, f32[1,128]{1,0:T(1,128)} %bitcast.5, bf16[2560,512]{1,0:T(8,128)(2,1)} %w_query.1, ...), custom_call_target="tpu_custom_call" | custom-call | tf_op jit(solution)/shard_map/pallas_call | solution.py:510
  24.1 1.3 %copy.20 = bf16[4,2,640]{2,1,0:T(2,128)(2,1)} copy(bf16[4,2,640]{2,1,0:T(2,128)(2,1)} %get-tuple-element.6) | data formatting | bytes 20480
  25.4 1.2 %copy.21 = bf16[4,2,128]{2,1,0:T(2,128)(2,1)} copy(bf16[4,2,128]{2,1,0:T(2,128)(2,1)} %get-tuple-element.7) | data formatting | bytes 4096
  26.7 1.2 %copy.22 = bf16[4,2,128]{2,1,0:T(2,128)(2,1)} copy(bf16[4,2,128]{2,1,0:T(2,128)(2,1)} %get-tuple-element.8) | data formatting | bytes 4096

commit v3 on v2

--- a/solution.py
+++ b/solution.py
@@ -160,7 +160,7 @@
                 w_out.at[:, pl.ds(start, cols)], w_out_parts.at[k], wo_sem.at[k]
             )
         )
-    for load in loads:
+    for load in loads[:3]:
         load.start()
 
     smalls[0].wait()
@@ -169,10 +169,14 @@
         for r in range(own):
             x_rows[r * steps + t : r * steps + t + 1, :] = block[r : r + 1, :]
     own_x = x_rows[...]
-    pieces = [own_x[:, c * HEAD : (c + 1) * HEAD] for c in range(chunks)]
     padding = x_parts.shape[1] // rows - chunks
-    pieces += [jnp.zeros((rows, HEAD), F32)] * padding
-    x_parts[my_mp] = jnp.concatenate(pieces, axis=0).astype(BF16)
+
+    def fold(wide):
+        pieces = [wide[:, c * HEAD : (c + 1) * HEAD] for c in range(chunks)]
+        pieces += [jnp.zeros((rows, HEAD), F32)] * padding
+        return jnp.concatenate(pieces, axis=0).astype(BF16)
+
+    x_parts[my_mp] = fold(own_x)
 
     pl.semaphore_wait(barrier, n_mp - 1 + n_seq - 1)
 
@@ -189,6 +193,8 @@
             )
         )
         x_copies[-1].start()
+    for load in loads[3:]:
+        load.start()
 
     for small in smalls[1:]:
         small.wait()
@@ -341,7 +347,6 @@
     stat_row = lax.broadcasted_iota(jnp.int32, (group, HEAD), 0)
     at_top = stat_lane == stat_row
     at_total = stat_lane == stat_row + HEAD // 2
-    stat_rows = st_out.shape[1]
 
     def partial_copies(k):
         there = {"seq": flip(my_seq, k, n_seq)}
@@ -385,9 +390,8 @@
             o_out[k, r] = mix.astype(BF16)
             spread = jnp.where(at_top, top, jnp.where(at_total, total, 0.0))
             lines.append(jnp.sum(spread, axis=0, keepdims=True))
-        blank = jnp.zeros((stat_rows - own, HEAD), F32)
-        for i, k in enumerate(ks):
-            st_out[k] = jnp.concatenate(lines[i * own : (i + 1) * own] + [blank], axis=0)
+        for line, (k, r, _, _) in zip(lines, jobs):
+            st_out[k, r : r + 1, :] = line
         for k in ks:
             for copy in partial_copies(k):
                 copy.start()
@@ -438,7 +442,7 @@
     y_copies = []
     for k in range(n_mp - 1, 0, -1):
         loads[5 + k].wait()
-        y_out[k] = jnp.dot(attended, w_out_parts[k], preferred_element_type=F32)
+        y_out[k] = fold(jnp.dot(attended, w_out_parts[k], preferred_element_type=F32))
         y_copies.append(
             pltpu.make_async_remote_copy(
                 src_ref=y_out.at[k],
@@ -452,20 +456,9 @@
         y_copies[-1].start()
     loads[5].wait()
     summed = jnp.dot(attended, w_out_parts[0], preferred_element_type=F32)
-    for copy in y_copies:
-        copy.wait_recv()
-    for k in range(1, n_mp):
-        summed = summed + y_in[k]
-    result = x_rows[...] + summed
-    for r in range(own):
-        for t in range(steps):
-            t_rows[t * own + r : t * own + r + 1, :] = result[
-                r * steps + t : r * steps + t + 1, :
-            ]
-    for t in range(steps):
-        hidden[t] = t_rows[t * own : (t + 1) * own, :].astype(BF16)
-
-    for copy in x_copies + y_copies:
+    summed = x_rows[...] + summed
+
+    for copy in x_copies:
         copy.wait_send()
 
     def drain(k, carry):
@@ -475,6 +468,35 @@
         return carry
 
     loop(1, n_seq, drain, 0)
+
+    for copy in y_copies:
+        copy.wait_recv()
+    for k in range(1, n_mp):
+        folded = y_in[k].astype(F32)
+        summed = summed + jnp.concatenate(
+            [folded[c * rows : (c + 1) * rows, :] for c in range(chunks)], axis=1
+        )
+    for r in range(own):
+        for t in range(steps):
+            t_rows[t * own + r : t * own + r + 1, :] = summed[
+                r * steps + t : r * steps + t + 1, :
+            ]
+    for t in range(steps):
+        hidden[t] = t_rows[t * own : (t + 1) * own, :].astype(BF16)
+    for copy in y_copies:
+        copy.wait_send()
+
+
+def write_out(*refs):
+    count = len(refs) // 2
+    sem = refs[-1]
+    copies = [
+        pltpu.make_async_copy(refs[i], refs[count + i], sem.at[i]) for i in range(count)
+    ]
+    for copy in copies:
+        copy.start()
+    for copy in copies:
+        copy.wait()
 
 
 def shards(n_seq, n_mp, *args):
@@ -503,16 +525,15 @@
     requests = req_len.shape[0]
     assert key_matrix.shape[1] == HEAD
     part_rows = -(-(rows * (cols // HEAD)) // 16) * 16
-    stat_rows = -(-own // 8) * 8
     vmem = pl.BlockSpec(memory_space=pltpu.VMEM)
     far = pl.BlockSpec(memory_space=pltpu.HBM)
     dma = pltpu.SemaphoreType.DMA
-    return pl.pallas_call(
+    results = pl.pallas_call(
         functools.partial(kernel, n_seq, n_mp),
         out_shape=(
-            jax.ShapeDtypeStruct(states.shape, BF16),
-            jax.ShapeDtypeStruct((steps, own, HEAD), BF16),
-            jax.ShapeDtypeStruct((steps, own, HEAD), BF16),
+            pltpu.VMEM(states.shape, BF16),
+            pltpu.VMEM((steps, own, HEAD), BF16),
+            pltpu.VMEM((steps, own, HEAD), BF16),
         ),
         in_specs=[far] * 14,
         out_specs=(vmem, vmem, vmem),
@@ -535,11 +556,11 @@
             pltpu.VMEM((n_seq, own, group, HEAD), BF16),
             pltpu.VMEM((n_seq, own, group, HEAD), BF16),
             pltpu.VMEM((n_seq, own, group, HEAD), BF16),
-            pltpu.VMEM((n_seq, stat_rows, HEAD), F32),
-            pltpu.VMEM((n_seq, stat_rows, HEAD), F32),
+            pltpu.VMEM((n_seq, own, HEAD), F32),
+            pltpu.VMEM((n_seq, own, HEAD), F32),
             pltpu.VMEM((rows, q_width), F32),
-            pltpu.VMEM((n_mp, rows, cols), F32),
-            pltpu.VMEM((n_mp, rows, cols), F32),
+            pltpu.VMEM((n_mp, part_rows, HEAD), BF16),
+            pltpu.VMEM((n_mp, part_rows, HEAD), BF16),
             pltpu.VMEM((rows, cols), F32),
             pltpu.SMEM((requests,), jnp.int32),
             pltpu.SMEM((requests,), jnp.int32),
@@ -578,6 +599,13 @@
         slot_block,
         slot_empty,
     )
+    return pl.pallas_call(
+        write_out,
+        out_shape=tuple(jax.ShapeDtypeStruct(x.shape, x.dtype) for x in results),
+        in_specs=[vmem] * 3,
+        out_specs=(far,) * 3,
+        scratch_shapes=[dma((3,))],
+    )(*results)
 
 
 def solution(mesh):

time: 28.2 us -> 25.8 us (0.915)
  local copies, waits for them, and re-layouts: 3.79 us -> 1.19 us
  Pallas kernels: 23.5 us -> 23.8 us
    unnamed x3 -> x6, local copies, waits for them, and re-layouts: 3.79 us -> 1.19 us
    pallas_call x1 -> x2, Pallas kernels: 23.5 us -> 23.8 us  [the longest x1 22.4 us: shards(): pl.pallas_call(functools.partial(kernel, n_seq, n_mp), out_shape=(pltpu.V...]
where the time goes in v3:
time: 25.8 us; the launch traced here: 25.6 us
  Pallas kernels  23.8 us (92%)
  local copies, waits for them, and re-layouts  1.19 us (5%)
  between operations  0.65 us (3%)
    pallas_call x1, Pallas kernels, shards(): pl.pallas_call(functools.partial(kernel, n_seq, n_mp), out_shape=(pltpu.V...  22.4 us
    pallas_call x1, Pallas kernels, shards(): pl.pallas_call(write_out, out_shape=tuple((jax.ShapeDtypeStruct(x.shape,...  1.33 us
    unnamed x6, local copies, waits for them, and re-layouts  1.19 us

profile of v3, /device:TPU:0, one launch (start us, length us, event | category | flops | bytes accessed | tf_op | source)
XLA Modules:
  0.0 25.6 jit_solution(2524449387123052028)
XLA Ops:
  0.6 22.4 %shard_map.157 = (bf16[4,2,640]{2,1,0:T(2,128)(2,1)S(1)}, bf16[4,2,128]{2,1,0:T(2,128)(2,1)S(1)}, bf16[4,2,128]{2,1,0:T(2,128)(2,1)S(1)}) custom-call(bf16[4,2,640]{2,1,0:T(2,128)(2,1)} %states_far.1, f32[20,128]{1,0:T(8,128)} %bitcast.3, f32[1,128]{1,0:T(1,128)} %bitcast.4, f32[1,128]{1,0:T(1,128)} %bitcast.5, bf16[2560,512]{1,0:T(8,128)(2,1)} %w_query.1, ...), custom_call_target="tpu_custom_call" | custom-call | tf_op jit(solution)/shard_map/pallas_call | solution.py:531
  23.1 0.0 copy-start
  23.1 0.6 %copy-done = bf16[4,2,640]{2,1,0:T(2,128)(2,1)} copy-done((bf16[4,2,640]{2,1,0:T(2,128)(2,1)}, bf16[4,2,640]{2,1,0:T(2,128)(2,1)S(1)}, u32[]{:S(2)}) %copy-start) | copy-done | bytes 10264
  23.7 0.0 copy-start.1
  23.7 0.0 copy-start.2
  23.7 0.6 %copy-done.1 = bf16[4,2,128]{2,1,0:T(2,128)(2,1)} copy-done((bf16[4,2,128]{2,1,0:T(2,128)(2,1)}, bf16[4,2,128]{2,1,0:T(2,128)(2,1)S(1)}, u32[]{:S(2)}) %copy-start.1) | copy-done | bytes 2072
  24.3 0.0 copy-done.2
  24.3 1.3 %shard_map.158 = (bf16[4,2,640]{2,1,0:T(2,128)(2,1)}, bf16[4,2,128]{2,1,0:T(2,128)(2,1)}, bf16[4,2,128]{2,1,0:T(2,128)(2,1)}) custom-call(bf16[4,2,640]{2,1,0:T(2,128)(2,1)} %copy-done, bf16[4,2,128]{2,1,0:T(2,128)(2,1)} %copy-done.1, bf16[4,2,128]{2,1,0:T(2,128)(2,1)} %copy-done.2), custom_call_target="tpu_custom_call" | custom-call | tf_op jit(solution)/shard_map/pallas_call | solution.py:602
Async XLA Ops:
  23.1 0.6 %copy-start = (bf16[4,2,640]{2,1,0:T(2,128)(2,1)}, bf16[4,2,640]{2,1,0:T(2,128)(2,1)S(1)}, u32[]{:S(2)}) copy-start(bf16[4,2,640]{2,1,0:T(2,128)(2,1)S(1)} %get-tuple-element.6.refs_0_) | copy-start | bytes 30724
  23.7 0.6 %copy-start.1 = (bf16[4,2,128]{2,1,0:T(2,128)(2,1)}, bf16[4,2,128]{2,1,0:T(2,128)(2,1)S(1)}, u32[]{:S(2)}) copy-start(bf16[4,2,128]{2,1,0:T(2,128)(2,1)S(1)} %get-tuple-element.7.refs_1_) | copy-start | bytes 6148
  23.7 0.6 %copy-start.2 = (bf16[4,2,128]{2,1,0:T(2,128)(2,1)}, bf16[4,2,128]{2,1,0:T(2,128)(2,1)S(1)}, u32[]{:S(2)}) copy-start(bf16[4,2,128]{2,1,0:T(2,128)(2,1)S(1)} %get-tuple-element.8.refs_2_) | copy-start | bytes 6148

commit v4 on v3

--- a/solution.py
+++ b/solution.py
@@ -57,7 +57,7 @@
     hidden,
     new_keys,
     new_values,
-    states,
+    x_raw,
     norm_gain,
     query_gain,
     key_gain,
@@ -66,7 +66,6 @@
     slot_block,
     slot_empty,
     x_rows,
-    x_parts,
     w_all,
     w_out_parts,
     k_all,
@@ -99,7 +98,7 @@
     y_send,
     y_recv,
 ):
-    steps, own, cols = states.shape
+    steps, own, cols = states_far.shape
     rows = steps * own
     chunks = cols // HEAD
     width = cols * n_mp
@@ -116,7 +115,7 @@
         pltpu.make_async_copy(source, target, small_sem.at[i])
         for i, (source, target) in enumerate(
             (
-                (states_far, states),
+                (states_far, x_raw.at[lax.axis_index("mp")]),
                 (req_len_far, req_len),
                 (slot_request_far, slot_request),
                 (slot_block_far, slot_block),
@@ -163,29 +162,21 @@
     for load in loads[:3]:
         load.start()
 
-    smalls[0].wait()
-    for t in range(steps):
-        block = states[t].astype(F32)
-        for r in range(own):
-            x_rows[r * steps + t : r * steps + t + 1, :] = block[r : r + 1, :]
-    own_x = x_rows[...]
-    padding = x_parts.shape[1] // rows - chunks
+    padding = y_out.shape[1] // rows - chunks
 
     def fold(wide):
         pieces = [wide[:, c * HEAD : (c + 1) * HEAD] for c in range(chunks)]
         pieces += [jnp.zeros((rows, HEAD), F32)] * padding
         return jnp.concatenate(pieces, axis=0).astype(BF16)
 
-    x_parts[my_mp] = fold(own_x)
-
     pl.semaphore_wait(barrier, n_mp - 1 + n_seq - 1)
 
     x_copies = []
     for k in range(n_mp - 1, 0, -1):
         x_copies.append(
             pltpu.make_async_remote_copy(
-                src_ref=x_parts.at[my_mp],
-                dst_ref=x_parts.at[my_mp],
+                src_ref=states_far,
+                dst_ref=x_raw.at[my_mp],
                 send_sem=x_send.at[k],
                 recv_sem=x_recv.at[k],
                 device_id={"mp": flip(my_mp, k, n_mp)},
@@ -196,7 +187,7 @@
     for load in loads[3:]:
         load.start()
 
-    for small in smalls[1:]:
+    for small in smalls:
         small.wait()
 
     owners = []
@@ -245,14 +236,15 @@
 
     for copy in x_copies:
         copy.wait_recv()
-    blocks = []
-    square = jnp.zeros((rows, HEAD), F32)
     for m in range(n_mp):
-        part = x_parts[m].astype(F32)
-        for c in range(chunks):
-            piece = part[c * rows : (c + 1) * rows, :]
-            blocks.append(piece)
-            square = square + piece * piece
+        for t in range(steps):
+            block = x_raw[m, t].astype(F32)
+            for r in range(own):
+                x_rows[r * steps + t : r * steps + t + 1, m * cols : (m + 1) * cols] = block[
+                    r : r + 1, :
+                ]
+    blocks = [x_rows[:, c * HEAD : (c + 1) * HEAD] for c in range(n_mp * chunks)]
+    square = sum(piece * piece for piece in blocks)
     mean = jnp.sum(square, axis=-1, keepdims=True) * (1.0 / width)
     factor = lax.rsqrt(mean + EPS)
     gains = norm_gain[...]
@@ -456,7 +448,8 @@
         y_copies[-1].start()
     loads[5].wait()
     summed = jnp.dot(attended, w_out_parts[0], preferred_element_type=F32)
-    summed = x_rows[...] + summed
+    own_start = pl.multiple_of(my_mp * cols, HEAD)
+    summed = x_rows[:, pl.ds(own_start, cols)] + summed
 
     for copy in x_copies:
         copy.wait_send()
@@ -538,7 +531,7 @@
         in_specs=[far] * 14,
         out_specs=(vmem, vmem, vmem),
         scratch_shapes=[
-            pltpu.VMEM(states.shape, BF16),
+            pltpu.VMEM((n_mp,) + states.shape, BF16),
             pltpu.VMEM((width // HEAD, HEAD), F32),
             pltpu.VMEM((1, HEAD), F32),
             pltpu.VMEM((1, HEAD), F32),
@@ -546,8 +539,7 @@
             pltpu.SMEM((slots,), jnp.int32),
             pltpu.SMEM((slots,), jnp.int32),
             pltpu.SMEM((slots,), jnp.int32),
-            pltpu.VMEM((rows, cols), F32),
-            pltpu.VMEM((n_mp, part_rows, HEAD), BF16),
+            pltpu.VMEM((rows, width), F32),
             pltpu.VMEM((width, q_width + 2 * HEAD), BF16),
             pltpu.VMEM((n_mp, q_width, cols), BF16),
             pltpu.VMEM((slots, block_len, HEAD), BF16),
@@ -605,6 +597,7 @@
         in_specs=[vmem] * 3,
         out_specs=(far,) * 3,
         scratch_shapes=[dma((3,))],
+        compiler_params=pltpu.CompilerParams(vmem_limit_bytes=1024 * 1024),
     )(*results)
 
 

time: 25.8 us -> 24.1 us (0.934)
  local copies, waits for them, and re-layouts: 1.19 us -> 0 us
  Pallas kernels: 23.8 us -> 23.3 us
    unnamed x6 -> x0, local copies, waits for them, and re-layouts: 1.19 us -> none
    pallas_call x1, Pallas kernels: 1.33 us -> 0.63 us  [shards(): pl.pallas_call(write_out, out_shape=tuple((jax.ShapeDtypeStruct(x.shape,...]
where the time goes in v4:
time: 24.1 us; the launch traced here: 23.9 us
  Pallas kernels  23.3 us (97%)
  between operations  0.64 us (3%)
    pallas_call x1, Pallas kernels, shards(): pl.pallas_call(functools.partial(kernel, n_seq, n_mp), out_shape=(pltpu.V...  22.6 us
    pallas_call x1, Pallas kernels, shards(): pl.pallas_call(write_out, out_shape=tuple((jax.ShapeDtypeStruct(x.shape,...  0.63 us

profile of v4, /device:TPU:0, one launch (start us, length us, event | category | flops | bytes accessed | tf_op | source)
XLA Modules:
  0.0 23.9 jit_solution(5045111225380772969)
XLA Ops:
  0.6 22.6 %shard_map.157 = (bf16[4,2,640]{2,1,0:T(2,128)(2,1)S(1)}, bf16[4,2,128]{2,1,0:T(2,128)(2,1)S(1)}, bf16[4,2,128]{2,1,0:T(2,128)(2,1)S(1)}) custom-call(bf16[4,2,640]{2,1,0:T(2,128)(2,1)} %states_far.1, f32[20,128]{1,0:T(8,128)} %bitcast.3, f32[1,128]{1,0:T(1,128)} %bitcast.4, f32[1,128]{1,0:T(1,128)} %bitcast.5, bf16[2560,512]{1,0:T(8,128)(2,1)} %w_query.1, ...), custom_call_target="tpu_custom_call" | custom-call | tf_op jit(solution)/shard_map/pallas_call | solution.py:524
  23.3 0.6 %shard_map.158 = (bf16[4,2,640]{2,1,0:T(2,128)(2,1)}, bf16[4,2,128]{2,1,0:T(2,128)(2,1)}, bf16[4,2,128]{2,1,0:T(2,128)(2,1)}) custom-call(bf16[4,2,640]{2,1,0:T(2,128)(2,1)S(1)} %get-tuple-element.6.refs_0_, bf16[4,2,128]{2,1,0:T(2,128)(2,1)S(1)} %get-tuple-element.7.refs_1_, bf16[4,2,128]{2,1,0:T(2,128)(2,1)S(1)} %get-tuple-element.8.refs_2_), custom_call_target="tpu_custom_call" | custom-call | tf_op jit(solution)/shard_map/pallas_call | solution.py:594

commit v5 on v4

--- a/solution.py
+++ b/solution.py
@@ -184,9 +184,6 @@
             )
         )
         x_copies[-1].start()
-    for load in loads[3:]:
-        load.start()
-
     for small in smalls:
         small.wait()
 
@@ -253,6 +250,8 @@
     ).astype(BF16)
     for load in loads[:3]:
         load.wait()
+    for load in loads[3:5]:
+        load.start()
     projected = jnp.dot(normed, w_all[...], preferred_element_type=F32)
 
     for h in range(heads):
@@ -293,6 +292,8 @@
 
     for load in loads[3:5]:
         load.wait()
+    for load in loads[5:]:
+        load.start()
 
     key_lane = lax.broadcasted_iota(jnp.int32, (group, block_len), 1)
     contract = (((1,), (1,)), ((), ()))

time: 24.1 us -> 24.1 us (level)
  no operation moved by 1% of the time
where the time goes in v5:
time: 24.1 us; the launch traced here: 23.9 us
  Pallas kernels  23.3 us (97%)
  between operations  0.64 us (3%)
    pallas_call x1, Pallas kernels, shards(): pl.pallas_call(functools.partial(kernel, n_seq, n_mp), out_shape=(pltpu.V...  22.6 us
    pallas_call x1, Pallas kernels, shards(): pl.pallas_call(write_out, out_shape=tuple((jax.ShapeDtypeStruct(x.shape,...  0.63 us

profile of v5, /device:TPU:0, one launch (start us, length us, event | category | flops | bytes accessed | tf_op | source)
XLA Modules:
  0.0 23.9 jit_solution(13299780786208646193)
XLA Ops:
  0.6 22.6 %shard_map.157 = (bf16[4,2,640]{2,1,0:T(2,128)(2,1)S(1)}, bf16[4,2,128]{2,1,0:T(2,128)(2,1)S(1)}, bf16[4,2,128]{2,1,0:T(2,128)(2,1)S(1)}) custom-call(bf16[4,2,640]{2,1,0:T(2,128)(2,1)} %states_far.1, f32[20,128]{1,0:T(8,128)} %bitcast.3, f32[1,128]{1,0:T(1,128)} %bitcast.4, f32[1,128]{1,0:T(1,128)} %bitcast.5, bf16[2560,512]{1,0:T(8,128)(2,1)} %w_query.1, ...), custom_call_target="tpu_custom_call" | custom-call | tf_op jit(solution)/shard_map/pallas_call | solution.py:525
  23.3 0.6 %shard_map.158 = (bf16[4,2,640]{2,1,0:T(2,128)(2,1)}, bf16[4,2,128]{2,1,0:T(2,128)(2,1)}, bf16[4,2,128]{2,1,0:T(2,128)(2,1)}) custom-call(bf16[4,2,640]{2,1,0:T(2,128)(2,1)S(1)} %get-tuple-element.6.refs_0_, bf16[4,2,128]{2,1,0:T(2,128)(2,1)S(1)} %get-tuple-element.7.refs_1_, bf16[4,2,128]{2,1,0:T(2,128)(2,1)S(1)} %get-tuple-element.8.refs_2_), custom_call_target="tpu_custom_call" | custom-call | tf_op jit(solution)/shard_map/pallas_call | solution.py:595
